TPU v7x, 512 devices: a whole 4x4x16 slice. The times are simulated.
512 devices in a mesh: wide: 64 (over y, z), narrow: 8 (over x, core).
Axes of the slice: x: 4, y: 4, z: 16, core: 2. Of those that a mesh axis runs over, the one named last changes fastest.
Arguments:
- images: float32 [2048, 3, 1024], P(('wide', 'narrow')), may hold values from -12 to 12
- block_slot: int32 [1024], replicated, may hold values from 0 to 1023, as said below
- pairs: int32 [512, 64, 2], P(('wide', 'narrow')), may hold values from 0 to 1023, as said below
Outputs:
- row_tiles: float32 [512, 64, 4], P(('wide', 'narrow'))
- col_tiles: float32 [512, 64, 4], P(('wide', 'narrow'))
Inputs may be any that keep to these rules, and one draw needn't show every extreme that they name: `block_slot`: a permutation of the block numbers. Storage slot s lies on device s // 2. For device d = w * 8 + n and slot j, block pairs[d, j, 0] is stored on device w * 8 + j // 8 and block pairs[d, j, 1] on device j * 8 + n; every block is the column block of some slot.
All inputs are finite; a program needn't handle non-finite values.
Results may differ from a plain program's by a relative error of at most 0.00002.
Values sent between devices are 32-bit elements; how exact they have to be, the bound alone decides.
No kernel may reach another device: no remote copies, remote signals or barrier semaphores. Data moves between devices by JAX's collectives and lax.ppermute only.
A program may use at most 64 MiB of HBM per device.

v0:
```python
import math

import jax
import jax.numpy as jnp
from jax import lax
from jax.sharding import PartitionSpec as P

BLOCK = 2
BLK_DEV = 2
CH = 3
SIDE = 32
LAYERS = 4
POS = 1024


SIGMA_W = 2.0
SIGMA_B = 0.1
PI_VALUE = math.pi


def shift_flat(values_in, offset):
    pad_shape = values_in.shape[:-1] + (abs(offset),)
    zeros_pad = jnp.zeros(pad_shape, values_in.dtype)
    if offset > 0:
        return jnp.concatenate([values_in[..., offset:], zeros_pad], -1)
    return jnp.concatenate([zeros_pad, values_in[..., :offset]], -1)


def box_mean(values_in):
    column = lax.rem(lax.iota(jnp.int32, values_in.shape[-1]), jnp.int32(SIDE))
    to_right = jnp.where(column < SIDE - 1, shift_flat(values_in, 1), 0.0)
    to_left = jnp.where(column > 0, shift_flat(values_in, -1), 0.0)
    row_sum = values_in + to_right + to_left
    return (row_sum + shift_flat(row_sum, SIDE) + shift_flat(row_sum, -SIDE)) / 9.0


def relu_expect(covariance, var_first, var_second):
    magnitude = jnp.sqrt(var_first * var_second)
    cosine = jnp.clip(covariance / magnitude, -1.0, 1.0)
    angle_rad = jnp.arccos(cosine)
    return magnitude * (jnp.sin(angle_rad) + (PI_VALUE - angle_rad) * cosine) / (2.0 * PI_VALUE)


def variance_maps(block_data):
    variance = SIGMA_W * box_mean(jnp.mean(block_data * block_data, axis=-2)) + SIGMA_B
    var_list = [variance]
    for level_idx in range(1, LAYERS):
        variance = SIGMA_W * box_mean(0.5 * variance) + SIGMA_B
        var_list.append(variance)
    return jnp.stack(var_list, axis=-2)


def pair_kernel(row_data, row_vars, col_data, col_vars):
    inner_sum = row_data[..., :, None, 0, :] * col_data[..., None, :, 0, :]
    for channel in range(1, CH):
        inner_sum = (
            inner_sum + row_data[..., :, None, channel, :] * col_data[..., None, :, channel, :]
        )
    covariance = SIGMA_W * box_mean(inner_sum / CH) + SIGMA_B
    for level_idx in range(LAYERS):
        after_relu = relu_expect(
            covariance, row_vars[..., :, None, level_idx, :], col_vars[..., None, :, level_idx, :]
        )
        if level_idx < LAYERS - 1:
            covariance = SIGMA_W * box_mean(after_relu) + SIGMA_B
    return SIGMA_W * jnp.mean(after_relu, axis=-1) + SIGMA_B


def peer_tiles(row_data, row_vars, col_data, col_vars):
    peer_count = row_data.shape[0]

    def grouped(array_in):
        return array_in.reshape((peer_count // 8, 8) + array_in.shape[1:])

    result = lax.map(
        lambda pieces: pair_kernel(pieces[0], pieces[1], pieces[2], pieces[3]),
        (grouped(row_data), grouped(row_vars), grouped(col_data), grouped(col_vars)),
    )
    return result.reshape((peer_count,) + result.shape[2:])


def lookup(table, wanted):
    matches = wanted[..., None] == lax.iota(jnp.int32, table.shape[0])
    return jnp.sum(jnp.where(matches, table, 0), axis=-1)


def shards(images, block_slot, pairs):
    wide_n = lax.axis_size("wide")
    narrow_n = lax.axis_size("narrow")
    per_narrow = wide_n // narrow_n
    blocks = images.reshape(BLK_DEV, BLOCK, CH, POS)
    wanted = pairs.reshape(wide_n, 2)
    slot_ids = lookup(block_slot, wanted)
    row_index = slot_ids[:, 0] % BLK_DEV + lax.iota(jnp.int32, wide_n) // per_narrow * BLK_DEV
    col_local = slot_ids[:, 1] % BLK_DEV
    requested = lax.all_to_all(col_local, "wide", split_axis=0, concat_axis=0, tiled=True)
    own_vars = variance_maps(blocks)
    near_images, near_vars = (
        lax.all_gather(blocks, "narrow", axis=0, tiled=True),
        lax.all_gather(own_vars, "narrow", axis=0, tiled=True),
    )
    row_data = jnp.take(near_images, row_index, axis=0)
    row_vars = jnp.take(near_vars, row_index, axis=0)
    out_images = jnp.take(blocks, requested, axis=0)
    out_vars = jnp.take(own_vars, requested, axis=0)
    pair_tiles = peer_tiles(
        row_data,
        row_vars,
        lax.all_to_all(out_images, "wide", split_axis=0, concat_axis=0, tiled=True),
        lax.all_to_all(out_vars, "wide", split_axis=0, concat_axis=0, tiled=True),
    )
    flipped = jnp.swapaxes(pair_tiles, 1, 2).reshape(wide_n, BLOCK * BLOCK)
    col_tiles = lax.all_to_all(flipped, "wide", split_axis=0, concat_axis=0, tiled=True)
    by_owner = pair_tiles.reshape(narrow_n, per_narrow, BLOCK * BLOCK)
    row_tiles = lax.all_to_all(by_owner, "narrow", split_axis=0, concat_axis=0, tiled=True)
    return (
        row_tiles.reshape(1, wide_n, BLOCK * BLOCK),
        col_tiles.reshape(1, wide_n, BLOCK * BLOCK),
    )


def solution(mesh):
    in_specs = (P(("wide", "narrow"), None, None), P(), P(("wide", "narrow"), None, None))
    out_specs = (P(("wide", "narrow"), None, None), P(("wide", "narrow"), None, None))
    return jax.shard_map(shards, mesh=mesh, in_specs=in_specs, out_specs=out_specs, check_vma=False)
```

profile of v0, /device:TPU:1, one launch (start us, length us, event | category | flops | bytes accessed | tf_op | source)
XLA Modules:
  0.0 326.4 jit_solution(16608247690880233304)
XLA Ops:
  0.6 0.9 select_reduce_fusion
  2.3 19.3 %all-to-all-start = ((s32[64,1,1]{2,1,0:T(1,128)}), s32[64,1,1]{2,1,0:T(1,128)S(1)}, u32[]{:S(2)}, u32[]{:S(2)}) async-start(s32[64,1,1]{2,1,0:T(1,128)} %copy.57), calls=%async_computation | async-start | bytes 65536 | tf_op jit(solution)/shard_map/all_to_all | solution.py:96
  21.6 0.8 reshape.195
  22.4 12.4 %all-to-all-done = s32[64,1,1]{2,1,0:T(1,128)S(1)} async-done(((s32[64,1,1]{2,1,0:T(1,128)}), s32[64,1,1]{2,1,0:T(1,128)S(1)}, u32[]{:S(2)}, u32[]{:S(2)}) %all-to-all-start) | async-done | bytes 288 | tf_op jit(solution)/shard_map/all_to_all | solution.py:96
  34.8 1.2 reduce.1
  36.1 2.2 gather_fusion.3
  38.3 2.0 broadcast_select_fusion
  40.4 5.6 %all-to-all-start.2 = ((f32[64,2,3,1024]{3,1,2,0:T(2,128)}), f32[64,2,3,1024]{3,1,2,0:T(2,128)}, u32[]{:S(2)}, u32[]{:S(2)}) async-start(f32[64,2,3,1024]{3,1,2,0:T(2,128)} %broadcast_select_fusion), calls=%async_computation.2 | async-start | bytes 3145728 | tf_op jit(solution)/shard_map/all_to_all | solution.py:109
  47.7 1.8 gather_fusion.1
  49.5 1.8 broadcast_select_fusion.1
  51.3 64.8 %all-to-all-done.2 = f32[64,2,3,1024]{3,1,2,0:T(2,128)} async-done(((f32[64,2,3,1024]{3,1,2,0:T(2,128)}), f32[64,2,3,1024]{3,1,2,0:T(2,128)}, u32[]{:S(2)}, u32[]{:S(2)}) %all-to-all-start.2) | async-done | bytes 1572896 | tf_op jit(solution)/shard_map/all_to_all | solution.py:109
  116.2 12.8 %all-to-all-start.1 = ((f32[64,2,4,1024]{3,2,1,0:T(4,128)}), f32[64,2,4,1024]{3,2,1,0:T(4,128)}, u32[]{:S(2)}, u32[]{:S(2)}) async-start(f32[64,2,4,1024]{3,2,1,0:T(4,128)} %broadcast_select_fusion.1), calls=%async_computation.1 | async-start | bytes 4194304 | tf_op jit(solution)/shard_map/all_to_all | solution.py:110
  129.1 14.5 %all_gather.6 = f32[16,2,4,1024]{3,2,1,0:T(4,128)S(1)} all-gather(f32[2,2,4,1024]{3,2,1,0:T(4,128)S(1)} %pad_maximum_fusion), channel_id=1, replica_groups=mesh['wide'=64,'narrow'=8] {'narrow'}, dimensions={0}, use_global_device_ids=true | all-gather | bytes 589824 | tf_op jit(solution)/shard_map/all_gather | solution.py:100
  143.6 3.0 gather_fusion
  146.7 13.1 %all_gather.7 = f32[16,2,3,1024]{3,1,2,0:T(2,128)S(1)} all-gather(f32[2,2,3,1024]{3,1,2,0:T(2,128)S(1)} %copy.58), channel_id=1, replica_groups=mesh['wide'=64,'narrow'=8] {'narrow'}, dimensions={0}, use_global_device_ids=true | all-gather | bytes 442368 | tf_op jit(solution)/shard_map/all_gather | solution.py:99
  159.8 2.2 gather_fusion.2
  162.0 1.9 copy_select_fusion.1
  164.0 1.4 copy_select_fusion
  165.4 55.2 %all-to-all-done.1 = f32[64,2,4,1024]{3,2,1,0:T(4,128)} async-done(((f32[64,2,4,1024]{3,2,1,0:T(4,128)}), f32[64,2,4,1024]{3,2,1,0:T(4,128)}, u32[]{:S(2)}, u32[]{:S(2)}) %all-to-all-start.1) | async-done | bytes 2097184 | tf_op jit(solution)/shard_map/all_to_all | solution.py:110
  220.6 68.5 %while.13 = (s32[]{:T(128)}, f32[8,8,2,2]{1,3,2,0:T(2,128)}, f32[8,8,2,4,1024]{4,1,2,3,0:T(8,128)S(1)}, f32[8,8,2,4,1024]{4,3,2,1,0:T(4,128)}, f32[8,8,2,3,1024]...) while((s32[]{:T(128)}, f32[8,8,2,2]{1,3,2,0:T(2,128)}, f32[8,8,2,4,1024]{4,1,2,3,0:T(8,128)S(1)}, ...), condition=%wide.region_4.5_spmd, body=%wide.region_2.4_spmd.sunk | while | flops 2919458 | bytes 14067549 | solution.py:75
  220.6 0.9 constant_dynamic-slice_fusion.4
  221.7 0.9 dynamic-slice_bitcast_fusion.4
  223.0 1.0 constant_dynamic-slice_fusion.5
  225.4 0.8 multiply_multiply_fusion.7
  226.5 0.8 multiply_multiply_fusion.8
  227.7 0.9 multiply_reduce_fusion.3
  229.2 0.9 constant_dynamic-slice_fusion.4
  230.2 0.9 dynamic-slice_bitcast_fusion.4
  231.6 1.0 constant_dynamic-slice_fusion.5
  235.1 0.8 multiply_multiply_fusion.8
  236.2 0.9 multiply_reduce_fusion.3
  237.8 0.9 constant_dynamic-slice_fusion.4
  238.8 0.9 dynamic-slice_bitcast_fusion.4
  240.1 1.0 constant_dynamic-slice_fusion.5
  242.5 0.8 multiply_multiply_fusion.7
  243.7 0.8 multiply_multiply_fusion.8
  244.8 0.9 multiply_reduce_fusion.3
  246.3 0.9 constant_dynamic-slice_fusion.4
  247.3 0.9 dynamic-slice_bitcast_fusion.4
  248.7 1.0 constant_dynamic-slice_fusion.5
  251.1 0.8 multiply_multiply_fusion.7
  252.2 0.8 multiply_multiply_fusion.8
  253.4 0.9 multiply_reduce_fusion.3
  254.9 0.9 constant_dynamic-slice_fusion.4
  255.9 0.9 dynamic-slice_bitcast_fusion.4
  257.3 1.0 constant_dynamic-slice_fusion.5
  260.8 0.8 multiply_multiply_fusion.8
  261.9 0.9 multiply_reduce_fusion.3
  263.5 0.9 constant_dynamic-slice_fusion.4
  264.5 0.9 dynamic-slice_bitcast_fusion.4
  265.8 1.0 constant_dynamic-slice_fusion.5
  270.5 0.9 multiply_reduce_fusion.3
  272.0 0.9 constant_dynamic-slice_fusion.4
  273.0 0.9 dynamic-slice_bitcast_fusion.4
  274.4 1.0 constant_dynamic-slice_fusion.5
  279.0 0.9 multiply_reduce_fusion.3
  280.6 0.9 constant_dynamic-slice_fusion.4
  281.6 0.9 dynamic-slice_bitcast_fusion.4
  282.9 1.0 constant_dynamic-slice_fusion.5
  287.6 0.9 multiply_reduce_fusion.3
  289.1 11.5 %all-to-all-start.3 = ((f32[8,8,4]{1,2,0:T(4,128)}), f32[8,8,4]{1,2,0:T(4,128)S(1)}, u32[]{:S(2)}, u32[]{:S(2)}) async-start(f32[8,8,4]{1,2,0:T(4,128)} %bitcast.30), calls=%async_computation.3 | async-start | bytes 32768 | tf_op jit(solution)/shard_map/all_to_all | solution.py:115
  302.2 3.1 all-to-all-done.3
  305.3 7.2 %all-to-all-start.4 = ((f32[64,1,4]{2,1,0:T(1,128)}), f32[64,1,4]{2,1,0:T(1,128)S(1)}, u32[]{:S(2)}, u32[]{:S(2)}) async-start(f32[64,1,4]{2,1,0:T(1,128)} %copy.66), calls=%async_computation.4 | async-start | bytes 65536 | tf_op jit(solution)/shard_map/all_to_all | solution.py:113
  313.2 12.6 %all-to-all-done.4 = f32[64,1,4]{2,1,0:T(1,128)S(1)} async-done(((f32[64,1,4]{2,1,0:T(1,128)}), f32[64,1,4]{2,1,0:T(1,128)S(1)}, u32[]{:S(2)}, u32[]{:S(2)}) %all-to-all-start.4) | async-done | bytes 1056 | tf_op jit(solution)/shard_map/all_to_all | solution.py:113
  (222 shorter events, 35.5 us)
Async XLA Ops:
  2.3 32.6 %all-to-all-start = ((s32[64,1,1]{2,1,0:T(1,128)}), s32[64,1,1]{2,1,0:T(1,128)S(1)}, u32[]{:S(2)}, u32[]{:S(2)}) async-start(s32[64,1,1]{2,1,0:T(1,128)} %copy.57), calls=%async_computation | async-start | bytes 65536 | tf_op jit(solution)/shard_map/all_to_all | solution.py:96
  40.4 5.7 %copy-start.1 = (f32[4,3,1024]{2,0,1:T(4,128)S(1)}, f32[4,3,1024]{2,0,1:T(4,128)}, u32[]{:S(2)}) copy-start(f32[4,3,1024]{2,0,1:T(4,128)} %param.5) | copy-start | bytes 147460
  40.4 75.8 %all-to-all-start.2 = ((f32[64,2,3,1024]{3,1,2,0:T(2,128)}), f32[64,2,3,1024]{3,1,2,0:T(2,128)}, u32[]{:S(2)}, u32[]{:S(2)}) async-start(f32[64,2,3,1024]{3,1,2,0:T(2,128)} %broadcast_select_fusion), calls=%async_computation.2 | async-start | bytes 3145728 | tf_op jit(solution)/shard_map/all_to_all | solution.py:109
  116.2 104.5 %all-to-all-start.1 = ((f32[64,2,4,1024]{3,2,1,0:T(4,128)}), f32[64,2,4,1024]{3,2,1,0:T(4,128)}, u32[]{:S(2)}, u32[]{:S(2)}) async-start(f32[64,2,4,1024]{3,2,1,0:T(4,128)} %broadcast_select_fusion.1), calls=%async_computation.1 | async-start | bytes 4194304 | tf_op jit(solution)/shard_map/all_to_all | solution.py:110
  162.0 2.0 copy-start
  289.1 16.2 %all-to-all-start.3 = ((f32[8,8,4]{1,2,0:T(4,128)}), f32[8,8,4]{1,2,0:T(4,128)S(1)}, u32[]{:S(2)}, u32[]{:S(2)}) async-start(f32[8,8,4]{1,2,0:T(4,128)} %bitcast.30), calls=%async_computation.3 | async-start | bytes 32768 | tf_op jit(solution)/shard_map/all_to_all | solution.py:115
  305.3 20.5 %all-to-all-start.4 = ((f32[64,1,4]{2,1,0:T(1,128)}), f32[64,1,4]{2,1,0:T(1,128)S(1)}, u32[]{:S(2)}, u32[]{:S(2)}) async-start(f32[64,1,4]{2,1,0:T(1,128)} %copy.66), calls=%async_computation.4 | async-start | bytes 65536 | tf_op jit(solution)/shard_map/all_to_all | solution.py:113
where the time goes:
time: 328 us; the launch traced here: 326 us
  waiting for transfers between devices  148 us (45%)
  starting transfers between devices  56.5 us (17%)
  other arithmetic  46.1 us (14%)
  local copies, waits for them, and re-layouts  45.9 us (14%)
  blocking collectives  27.7 us (8%)
    all_to_all x1, waiting for transfers between devices, shards(): lax.all_to_all(out_images, 'wide', split_axis=0, concat_axis=0, tiled=True)  64.8 us
    all_to_all x1, waiting for transfers between devices, shards(): lax.all_to_all(out_vars, 'wide', split_axis=0, concat_axis=0, tiled=True)  55.2 us
    div x24, other arithmetic, relu_expect(): magnitude * (jnp.sin(angle_rad) + (PI_VALUE - angle_rad) * cosine)  20 us
    all_to_all x1, starting transfers between devices, shards(): lax.all_to_all(col_local, 'wide', split_axis=0, concat_axis=0, tiled=True)  19.3 us
    dynamic_slice x32, local copies, waits for them, and re-layouts, peer_tiles(): lax.map(lambda pieces: pair_kernel(pieces[0], pieces[1], pieces[2], piece...  17.1 us
    all_gather x1, blocking collectives, shards(): lax.all_gather(own_vars, 'narrow', axis=0, tiled=True)  14.5 us
    all_gather x1, blocking collectives, shards(): lax.all_gather(blocks, 'narrow', axis=0, tiled=True)  13.1 us
    all_to_all x1, starting transfers between devices, shards(): lax.all_to_all(out_vars, 'wide', split_axis=0, concat_axis=0, tiled=True)  12.8 us
  transfers between devices with their start and end apart: 5, of which 5 were waited for; matrix products, arithmetic and copies ran while one was open for 5% of the time, Pallas kernels for 0%

commit v1 on v0

v1 whole, which is shorter than its diff:
```python
import math

import jax
import jax.numpy as jnp
from jax import lax
from jax.experimental import pallas as pl
from jax.experimental.pallas import tpu as pltpu
from jax.sharding import PartitionSpec as P

CH = 3
LAYERS = 4
POS = 1024
SIGMA_B = 0.1
BOTH = ("wide", "narrow")

IMG_ROWS = 96
ROWS = 104

X_SCALE = math.sqrt(2.0 / 27.0)
S_SCALE = math.sqrt(1.0 / (9.0 * math.pi))
TILE_SCALE = 9.0 / POS

H_POLY = (
    0.9428086134122584,
    0.04716169007693601,
    0.007401889707478926,
    0.002302233746421043,
    -0.00029199724221271717,
    0.0006175274818372866,
)


def flat(A, L, N):
    return (A * 8 + L) * 8 + N


def to_worker():
    return [
        (flat(a, l, q), flat(q, l ^ (4 * ((a ^ q) & 1)), a))
        for a in range(8)
        for l in range(8)
        for q in range(8)
    ]


def low_groups():
    return [[a * 8 + l for l in range(8)] for a in range(8)]


def return_groups():
    groups = []
    for n in range(8):
        for m in range(n + 1, 8):
            groups.append([flat(n, l, m) for l in range(8)] + [flat(m, l, n) for l in range(8)])
    for n in range(0, 8, 2):
        groups.append([flat(n, l, n) for l in range(8)] + [flat(n + 1, l, n + 1) for l in range(8)])
    return groups


def lane_iota(rows=8):
    return lax.broadcasted_iota(jnp.int32, (rows, 128), 1)


def sub_iota():
    return lax.broadcasted_iota(jnp.int32, (8, 128), 0)


def pack_kernel(images_ref, table_ref, pairs_ref, out_ref):
    wanted = pairs_ref[...]
    low = jnp.broadcast_to(wanted & 127, (8, 128))
    found = jnp.take_along_axis(table_ref[...], low, axis=1)
    mine = jnp.where(sub_iota() == jnp.broadcast_to(wanted >> 7, (8, 128)), found & 1, 0)
    local = jnp.sum(mine.astype(jnp.float32), axis=0, keepdims=True)
    for image in range(4):
        for channel in range(CH):
            for part in range(8):
                row = image * 24 + channel * 8 + part
                out_ref[0, row : row + 1, :] = (
                    images_ref[image, channel : channel + 1, part * 128 : (part + 1) * 128] * X_SCALE
                )
    out_ref[0, IMG_ROWS:ROWS, :] = jnp.broadcast_to(local, (8, 128))
    for peer in range(1, 8):
        out_ref[peer] = out_ref[0]


def relay_kernel(own_ref, near_ref, out_ref):
    out_ref[:IMG_ROWS, :] = own_ref[0, :IMG_ROWS, :]
    for n in range(8):
        out_ref[IMG_ROWS + n : IMG_ROWS + n + 1, :] = near_ref[n, 0:1, :]


def box_sum(x, masks):
    first_row, last_row, first_col, last_col = masks
    above = jnp.where(first_row, 0.0, pltpu.roll(x[3], 1, 0))
    below = jnp.where(last_row, 0.0, pltpu.roll(x[0], 7, 0))
    top, bottom = x[0] + x[1], x[2] + x[3]
    sums = [top + above, top + x[2], bottom + x[1], bottom + below]
    return [
        t + jnp.where(first_col, 0.0, pltpu.roll(t, 1, 1)) + jnp.where(last_col, 0.0, pltpu.roll(t, 127, 1))
        for t in sums
    ]


def tile_kernel(col_ref, row_ref, rows_out, cols_out, xr, xc, rr, rc, sr, sc, ta, tb, info, sem):
    high, near = lax.axis_index("wide") // 8, lax.axis_index("narrow")
    place = lax.axis_index("wide") % 8
    turn = ((high ^ near) & 1) * 4
    base = high * 16 + place * 2
    copy = pltpu.make_async_copy(row_ref.at[:, pl.ds(IMG_ROWS, 8), :], info, sem)
    copy.start()

    lane, sub = lane_iota(), sub_iota()
    column = lane & 31
    masks = (sub == 0, sub == 7, column == 0, column == 31)

    def prepare(source, block, x_out, r_out, s_out, first_image):
        device, local = block // 2, block % 2
        square = [None] * 4
        for channel in range(CH):
            start = pl.multiple_of(local * 48 + channel * 8, 8)
            one = source[device, pl.ds(start, 8), :]
            two = source[device, pl.ds(pl.multiple_of(start + 24, 8), 8), :]
            for v in range(4):
                index = column + 32 * v
                x = jnp.where(
                    first_image,
                    jnp.take_along_axis(one, index, axis=1),
                    jnp.take_along_axis(two, index, axis=1),
                )
                x_out[block, channel * 4 + v] = x
                square[v] = x * x if channel == 0 else square[v] + x * x
        variance = [b + SIGMA_B for b in box_sum(square, masks)]
        for level in range(LAYERS):
            for v in range(4):
                root = jnp.sqrt(variance[v])
                r_out[block, level * 4 + v] = 1.0 / root
                s_out[block, level * 4 + v] = root * S_SCALE
            if level < LAYERS - 1:
                variance = [b * (1.0 / 9.0) + SIGMA_B for b in box_sum(variance, masks)]

    def prepare_both(block, carry):
        prepare(row_ref, block, xr, rr, sr, lane < 64)
        prepare(col_ref, block, xc, rc, sc, (lane & 32) == 0)
        return carry

    lax.fori_loop(0, 16, prepare_both, 0)
    copy.wait()

    def one_pair(l, n):
        place_l = l ^ turn
        rb = place_l * 2 + info[place_l, n, base].astype(jnp.int32)
        cb = n * 2 + info[place_l, n, base + 1].astype(jnp.int32)
        products = []
        for v in range(4):
            t = xr[rb, v] * xc[cb, v]
            for channel in range(1, CH):
                t = t + xr[rb, channel * 4 + v] * xc[cb, channel * 4 + v]
            products.append(t)
        covariance = [b + SIGMA_B for b in box_sum(products, masks)]
        for level in range(LAYERS):
            relu = []
            for v in range(4):
                at = level * 4 + v
                cosine = covariance[v] * (rr[rb, at] * rc[cb, at])
                w = jnp.maximum(1.0 - jnp.abs(cosine), 1e-30)
                poly = H_POLY[-1] * w + H_POLY[-2]
                for coefficient in H_POLY[-3::-1]:
                    poly = poly * w + coefficient
                h = (w * w) * lax.rsqrt(w) * poly + math.pi * jnp.minimum(jnp.maximum(cosine, 0.0), 1.0)
                relu.append(h * (sr[rb, at] * sc[cb, at]))
            if level < LAYERS - 1:
                covariance = [b + SIGMA_B for b in box_sum(relu, masks)]
        total = jnp.sum((relu[0] + relu[1]) + (relu[2] + relu[3]), axis=0, keepdims=True)
        ta[pl.ds(n * 8 + l, 1), :] = total
        tb[pl.ds(l * 8 + n, 1), :] = total

    def some_pairs(step, carry):
        for u in range(4):
            one_pair(step // 2, (step % 2) * 4 + u)
        return carry

    lax.fori_loop(0, 16, some_pairs, 0)

    def gathered(ref, index):
        out = jnp.zeros((8, 128), jnp.float32)
        for g in range(8):
            t = ref[g * 8 : g * 8 + 8, :]
            for shift in (1, 2, 4, 8, 16):
                t = t + pltpu.roll(t, 128 - shift, 1)
            out = jnp.where(lane >> 2 == g, jnp.take_along_axis(t, index, axis=1), out)
        return out * TILE_SCALE + SIGMA_B

    rows = gathered(ta, (lane & 3) * 32)
    rows_out[0:8, :] = rows
    rows_out[8:16, :] = rows
    cols_out[...] = gathered(tb, (lane & 1) * 64 + ((lane >> 1) & 1) * 32)


def place_kernel(rows_ref, cols_ref, rows_out, cols_out):
    high, near = lax.axis_index("wide") // 8, lax.axis_index("narrow")
    half = jnp.where(high == near, high & 1, jnp.where(high < near, 1, 0))
    rows = rows_ref[pl.ds(pl.multiple_of(half * 8, 8), 8), :]
    cols = cols_ref[...]
    for g in range(8):
        shift = (128 - 4 * g) % 128
        rows_out[0, g * 8 : g * 8 + 8, :] = (pltpu.roll(rows, shift, 1) if shift else rows)[:, :4]
        cols_out[0, pl.ds(g, 8, stride=8), :] = (pltpu.roll(cols, shift, 1) if shift else cols)[:, :4]


def f32(*shape):
    return jax.ShapeDtypeStruct(shape, jnp.float32)


def whole(count):
    return [pl.BlockSpec(memory_space=pltpu.VMEM)] * count


def params():
    return pltpu.CompilerParams(vmem_limit_bytes=32 * 1024 * 1024)


def shards(images, block_slot, pairs):
    packed = pl.pallas_call(
        pack_kernel,
        out_shape=f32(8, ROWS, 128),
        in_specs=whole(3),
        out_specs=pl.BlockSpec(memory_space=pltpu.VMEM),
        compiler_params=params(),
    )(images, block_slot.reshape(8, 128), pairs.reshape(1, 128))
    near = lax.all_to_all(packed, "narrow", split_axis=0, concat_axis=0, tiled=True)
    relayed = pl.pallas_call(
        relay_kernel,
        out_shape=f32(ROWS, 128),
        grid=(1,),
        in_specs=[
            pl.BlockSpec((1, ROWS, 128), lambda i: (0, 0, 0)),
            pl.BlockSpec((8, 8, 128), lambda i: (0, IMG_ROWS // 8, 0)),
        ],
        out_specs=pl.BlockSpec((ROWS, 128), lambda i: (0, 0)),
        compiler_params=params(),
    )(packed, near)
    moved = lax.ppermute(relayed, BOTH, to_worker())
    far = lax.all_to_all(
        jnp.broadcast_to(moved[None], (8, ROWS, 128)),
        "wide",
        split_axis=0,
        concat_axis=0,
        tiled=True,
        axis_index_groups=low_groups(),
    )
    row_send, col_send = pl.pallas_call(
        tile_kernel,
        out_shape=(f32(16, 128), f32(8, 128)),
        in_specs=whole(2),
        out_specs=tuple(whole(2)),
        scratch_shapes=[
            pltpu.VMEM((16, 4 * CH, 8, 128), jnp.float32),
            pltpu.VMEM((16, 4 * CH, 8, 128), jnp.float32),
            pltpu.VMEM((16, 4 * LAYERS, 8, 128), jnp.float32),
            pltpu.VMEM((16, 4 * LAYERS, 8, 128), jnp.float32),
            pltpu.VMEM((16, 4 * LAYERS, 8, 128), jnp.float32),
            pltpu.VMEM((16, 4 * LAYERS, 8, 128), jnp.float32),
            pltpu.VMEM((64, 128), jnp.float32),
            pltpu.VMEM((64, 128), jnp.float32),
            pltpu.SMEM((8, 8, 128), jnp.float32),
            pltpu.SemaphoreType.DMA,
        ],
        compiler_params=params(),
    )(near, far)
    row_got = lax.all_to_all(
        row_send, BOTH, split_axis=0, concat_axis=0, tiled=True, axis_index_groups=return_groups()
    )
    col_got = lax.all_to_all(col_send, "narrow", split_axis=0, concat_axis=0, tiled=True)
    return pl.pallas_call(
        place_kernel,
        out_shape=(f32(1, 64, 4), f32(1, 64, 4)),
        in_specs=whole(2),
        out_specs=tuple(whole(2)),
        compiler_params=params(),
    )(row_got, col_got)


def solution(mesh):
    spec = P(BOTH, None, None)
    return jax.shard_map(
        shards, mesh=mesh, in_specs=(spec, P(), spec), out_specs=(spec, spec), check_vma=False
    )
```

time: 328 us -> 116 us (0.35)
  the two profiles are of different devices: /device:TPU:1 before, /device:TPU:5 now
where the time goes in v1:
time: 116 us
  blocking collectives  77.1 us (66%)
  Pallas kernels  18.9 us (16%)
  starting transfers between devices  14.3 us (12%)
  local copies, waits for them, and re-layouts  2.93 us (3%)
  waiting for transfers between devices  2.1 us (2%)
    all_to_all x1, blocking collectives, shards(): lax.all_to_all(jnp.broadcast_to(moved[None], (8, ROWS, 128)), 'wide', spl...  28.2 us
    all_to_all x1, blocking collectives, shards(): lax.all_to_all(row_send, BOTH, split_axis=0, concat_axis=0, tiled=True, a...  27.3 us
    pallas_call x1, Pallas kernels, shards(): pl.pallas_call(tile_kernel, out_shape=(f32(16, 128), f32(8, 128)), in_spe...  18.7 us
    all_to_all x1, blocking collectives, shards(): lax.all_to_all(packed, 'narrow', split_axis=0, concat_axis=0, tiled=True)  14.6 us
    ppermute x1, starting transfers between devices, shards(): moved = lax.ppermute(relayed, BOTH, to_worker())  14.3 us
    all_to_all x1, blocking collectives, shards(): lax.all_to_all(col_send, 'narrow', split_axis=0, concat_axis=0, tiled=True)  6.92 us
  transfers between devices with their start and end apart: 1, of which 1 were waited for; matrix products, arithmetic and copies ran while one was open for 0% of the time, Pallas kernels for 0%

profile of v1, /device:TPU:5, one launch (start us, length us, event | category | flops | bytes accessed | tf_op | source)
XLA Modules:
  0.0 116.0 jit_solution(2694641752823912223)
XLA Ops:
  0.6 0.0 copy-start.1
  0.6 0.8 copy.13
  1.4 0.1 reshape.16.pairs_ref
  1.6 0.0 copy-done.1
  1.6 0.0 copy-start
  1.6 0.6 copy-done
  2.3 0.1 shard_map.50.own_ref
  2.3 14.6 %all_to_all.32.near_ref.col_ref = f32[8,104,128]{2,1,0:T(8,128)S(1)} all-to-all(f32[8,104,128]{2,1,0:T(8,128)S(1)} %shard_map.50.own_ref), channel_id=1, replica_groups=mesh['wide'=64,'narrow'=8] {'narrow'}, dimensions={0} | all-to-all | bytes 851968 | tf_op jit(solution)/shard_map/all_to_all | solution.py:230
  17.0 14.3 %collective-permute-start = (f32[104,128]{1,0:T(8,128)S(1)}, f32[104,128]{1,0:T(8,128)S(1)}, u32[]{:S(2)}, u32[]{:S(2)}) collective-permute-start(f32[104,128]{1,0:T(8,128)S(1)} %shard_map.51), channel_id=1, source_target_pairs={{0,0},{1,96},{2,128},{3,224},{4,256},{5,352},{6,384},{7,480},{8,8}... | collective-permute-start | bytes 159752 | tf_op jit(solution)/shard_map/ppermute | solution.py:242
  31.3 2.1 %collective-permute-done = f32[104,128]{1,0:T(8,128)S(1)} collective-permute-done((f32[104,128]{1,0:T(8,128)S(1)}, f32[104,128]{1,0:T(8,128)S(1)}, u32[]{:S(2)}, u32[]{:S(2)}) %collective-permute-start) | collective-permute-done | bytes 53280 | tf_op jit(solution)/shard_map/ppermute | solution.py:242
  33.5 28.2 %all_to_all.33.row_ref = f32[8,104,128]{2,1,0:T(8,128)S(1)} all-to-all(f32[8,104,128]{2,1,0:T(8,128)S(1)} %broadcast_in_dim.2), channel_id=1, replica_groups={{0,8,16,24,32,40,48,56},{64,72,80,88,96,104,112,120},{128,136,144,152,1..., dimensions={0} | all-to-all | bytes 851968 | tf_op jit(solution)/shard_map/all_to_all | solution.py:243
  61.7 18.7 %shard_map.52 = (f32[16,128]{1,0:T(8,128)S(1)}, f32[8,128]{1,0:T(8,128)S(1)}) custom-call(f32[8,104,128]{2,1,0:T(8,128)S(1)} %all_to_all.32.near_ref.col_ref, f32[8,104,128]{2,1,0:T(8,128)S(1)} %all_to_all.33.row_ref), custom_call_target="tpu_custom_call" | custom-call | tf_op jit(solution)/shard_map/pallas_call | solution.py:251
  80.4 6.9 %all_to_all.34 = f32[8,1,128]{2,1,0:T(1,128)S(1)} all-to-all(f32[8,1,128]{2,1,0:T(1,128)S(1)} %bitcast.13), channel_id=1, replica_groups=mesh['wide'=64,'narrow'=8] {'narrow'}, dimensions={0} | all-to-all | bytes 8192 | tf_op jit(solution)/shard_map/all_to_all | solution.py:273
  87.3 27.3 %all_to_all.35 = f32[16,1,128]{2,1,0:T(1,128)S(1)} all-to-all(f32[16,1,128]{2,1,0:T(1,128)S(1)} %bitcast.11), channel_id=1, replica_groups={{1,9,17,25,33,41,49,57,64,72,80,88,96,104,112,120},{2,10,18,26,34,42,50..., dimensions={0} | all-to-all | bytes 16384 | tf_op jit(solution)/shard_map/all_to_all | solution.py:270
  114.6 0.1 shard_map.53
  114.7 0.7 copy.17
  115.4 0.7 copy.18
  (3 shorter events, 0.1 us)
Async XLA Ops:
  0.6 0.9 copy-start.1
  1.6 0.7 copy-start
  17.0 16.4 %collective-permute-start = (f32[104,128]{1,0:T(8,128)S(1)}, f32[104,128]{1,0:T(8,128)S(1)}, u32[]{:S(2)}, u32[]{:S(2)}) collective-permute-start(f32[104,128]{1,0:T(8,128)S(1)} %shard_map.51), channel_id=1, source_target_pairs={{0,0},{1,96},{2,128},{3,224},{4,256},{5,352},{6,384},{7,480},{8,8}... | collective-permute-start | bytes 159752 | tf_op jit(solution)/shard_map/ppermute | solution.py:242

commit v2 on v1

v2 whole, which is shorter than its diff:
```python
import math

import jax
import jax.numpy as jnp
from jax import lax
from jax.experimental import pallas as pl
from jax.experimental.pallas import tpu as pltpu
from jax.sharding import PartitionSpec as P

CH = 3
LAYERS = 4
POS = 1024
SIGMA_B = 0.1
BOTH = ("wide", "narrow")

IMG_ROWS = 96
ROWS = 104

X_SCALE = math.sqrt(2.0 / 27.0)
H_SCALE = 1.0 / (9.0 * math.pi)
H_LINE = math.pi * H_SCALE
TILE_SCALE = 9.0 / POS

H_POLY = tuple(
    H_SCALE * value
    for value in (
    0.9428086134122584,
    0.04716169007693601,
    0.007401889707478926,
    0.002302233746421043,
    -0.00029199724221271717,
    0.0006175274818372866,
    )
)


def flat(A, L, N):
    return (A * 8 + L) * 8 + N


def worker_narrow(a, q):
    return (2 * (q // 2) + 2 - a // 2) % 4 * 2 + a % 2


def worker_low(l, turn, slot):
    if not turn:
        return l ^ (4 * slot)
    if (l & 1) == slot:
        return ((l >> 1) + 3) & 3
    return 4 + (((l >> 1) + 1) & 3)


def row_routes(slot):
    return [
        (flat(a, l, q), flat(q, worker_low(l, (a ^ q) & 1, slot), worker_narrow(a, q)))
        for a in range(8)
        for l in range(8)
        for q in range(8)
    ]


def low_groups():
    return [[g * 4 + l for l in range(4)] for g in range(16)]


def lane_iota(rows=8):
    return lax.broadcasted_iota(jnp.int32, (rows, 128), 1)


def sub_iota():
    return lax.broadcasted_iota(jnp.int32, (8, 128), 0)


def pack_kernel(images_ref, table_ref, pairs_ref, out_ref, rows, wide):
    lane = lane_iota()
    wide[...] = jnp.zeros((8, 128), jnp.int32)
    wide[0:2, 0:64] = pairs_ref[...]
    slots = wide[...]
    wanted = jnp.where(lane < 64, slots[0:1, :], pltpu.roll(slots, 64, 1)[1:2, :])
    found = jnp.take_along_axis(table_ref[...], wanted & 127, axis=1)
    mine = jnp.where(sub_iota() == wanted >> 7, found & 1, 0)
    out_ref[0, IMG_ROWS:, :] = jnp.broadcast_to(jnp.sum(mine.astype(jnp.float32), axis=0, keepdims=True), (8, 128))
    for channel in range(CH):
        for part in range(8):
            values = images_ref[channel, :, part * 128 : (part + 1) * 128] * X_SCALE
            for image in range(4):
                rows[image * CH + channel, part : part + 1, :] = values[image : image + 1, :]
    index = (lane & 64) // 2 + (lane & 31)
    for block in range(2):
        for channel in range(CH):
            for u in range(2):
                one, two = (
                    jnp.take_along_axis(rows[(block * 2 + i) * CH + channel], index + 64 * u, axis=1)
                    for i in range(2)
                )
                start = ((block * CH + channel) * 2 + u) * 8
                out_ref[0, start : start + 8, :] = jnp.where((lane & 32) == 0, one, two)
    for peer in range(1, 8):
        out_ref[peer] = out_ref[0]


def relay_kernel(own_ref, near_ref, out_ref):
    out_ref[:IMG_ROWS, :] = own_ref[0, :IMG_ROWS, :]
    for n in range(8):
        out_ref[IMG_ROWS + n : IMG_ROWS + n + 1, :] = near_ref[n, IMG_ROWS : IMG_ROWS + 1, :]


def spread_kernel(first_ref, second_ref, out_ref):
    for peer in range(4):
        out_ref[peer, 0] = first_ref[...]
        out_ref[peer, 1] = second_ref[...]


def box_sum(x, masks):
    first_row, last_row, first_col, last_col = masks
    above = jnp.where(first_row, 0.0, pltpu.roll(x[3], 1, 0))
    below = jnp.where(last_row, 0.0, pltpu.roll(x[0], 7, 0))
    top, bottom = x[0] + x[1], x[2] + x[3]
    sums = [top + above, top + x[2], bottom + x[1], bottom + below]
    return [
        t + jnp.where(first_col, 0.0, pltpu.roll(t, 1, 1)) + jnp.where(last_col, 0.0, pltpu.roll(t, 127, 1))
        for t in sums
    ]


def constants():
    lane, sub = lane_iota(), sub_iota()
    column = lane & 31
    masks = (sub == 0, sub == 7, column == 0, column == 31)
    return lane, masks, (lane & 64) // 2 + column, (lane & 32) + column


def prepare(read, block, local, x_out, v_out, index, masks):
    square = [None] * 4
    for channel in range(CH):
        for v in range(4):
            tile = read(local * 48 + channel * 16 + (v // 2) * 8)
            x = jnp.take_along_axis(tile, index + 64 * (v % 2), axis=1)
            x_out[block, channel * 4 + v] = x
            square[v] = x * x if channel == 0 else square[v] + x * x
    for v, b in enumerate(box_sum(square, masks)):
        v_out[block, v] = b + SIGMA_B


def deepen(block, v_out, level, masks):
    variance = [v_out[block, (level - 1) * 4 + v] for v in range(4)]
    for v, b in enumerate(box_sum(variance, masks)):
        v_out[block, level * 4 + v] = b * (1.0 / 9.0) + SIGMA_B


def pair_sums(blocks, xr, xc, vr, vc, masks):
    found = []
    for rb, cb in blocks:
        products = []
        for v in range(4):
            t = xr[rb, v] * xc[cb, v]
            for channel in range(1, CH):
                t = t + xr[rb, channel * 4 + v] * xc[cb, channel * 4 + v]
            products.append(t)
        found.append((rb, cb, products))
    for level in range(LAYERS):
        nexts = []
        for rb, cb, products in found:
            covariance = [b + SIGMA_B for b in box_sum(products, masks)]
            relu = []
            for v in range(4):
                at = level * 4 + v
                square = vr[rb, at] * vc[cb, at]
                inverse = lax.rsqrt(square)
                cosine = covariance[v] * inverse
                w = jnp.maximum(1.0 - jnp.abs(cosine), 1e-30)
                poly = H_POLY[-1] * w + H_POLY[-2]
                for coefficient in H_POLY[-3::-1]:
                    poly = poly * w + coefficient
                h = (w * w) * lax.rsqrt(w) * poly + H_LINE * jnp.minimum(jnp.maximum(cosine, 0.0), 1.0)
                relu.append(h * (square * inverse))
            nexts.append((rb, cb, relu))
        found = nexts
    return [
        jnp.sum((relu[0] + relu[1]) + (relu[2] + relu[3]), axis=0, keepdims=True) for rb, cb, relu in found
    ]


def col_kernel(near_ref, xc, vc):
    lane, masks, by_row, by_col = constants()

    def some(step, carry):
        for u in range(8):
            device = step * 4 + u // 2
            read = lambda start: near_ref[device, start : start + 8, :]
            prepare(read, step * 8 + u, u % 2, xc, vc, by_col, masks)
        return carry

    lax.fori_loop(0, 2, some, 0)
    for level in range(1, LAYERS):

        def deeper(step, carry):
            for u in range(8):
                deepen(step * 8 + u, vc, level, masks)
            return carry

        lax.fori_loop(0, 2, deeper, 0)


def choice_lane():
    return lax.axis_index("wide")


def own_kernel(first_ref, second_ref, xc, vc, sums_out, xr, vr, info, sems):
    base = choice_lane()
    copies = []
    for slot, ref in enumerate((first_ref, second_ref)):
        copies.append(pltpu.make_async_copy(ref.at[pl.ds(IMG_ROWS, 8), :], info.at[slot], sems.at[slot]))
        copies[-1].start()
    lane, masks, by_row, by_col = constants()
    for slot, ref in enumerate((first_ref, second_ref)):
        for local in range(2):
            prepare(lambda start: ref[start : start + 8, :], slot * 2 + local, local, xr, vr, by_row, masks)
    for level in range(1, LAYERS):
        for block in range(4):
            deepen(block, vr, level, masks)
    for copy in copies:
        copy.wait()

    def some_pairs(slot, carry):
        blocks = []
        for n in range(8):
            rb = slot * 2 + info[slot, n, base].astype(jnp.int32)
            blocks.append((rb, n * 2 + info[slot, n, base + 64].astype(jnp.int32)))
        for n, total in enumerate(pair_sums(blocks, xr, xc, vr, vc, masks)):
            sums_out[pl.ds(slot * 8 + n, 1), :] = total
        return carry

    lax.fori_loop(0, 2, some_pairs, 0)


def tile_kernel(far_ref, own_ref, xc, vc, tiles_out, xr, vr, sums, info, sem):
    high, near = lax.axis_index("wide") // 8, lax.axis_index("narrow")
    place = lax.axis_index("wide") % 8
    turn = ((high ^ near) & 1) == 1
    half, mine = place >> 2, place & 3
    base = choice_lane()
    copy = pltpu.make_async_copy(far_ref.at[:, :, pl.ds(IMG_ROWS, 8), :], info, sem)
    copy.start()
    lane, masks, by_row, by_col = constants()

    def row_at(p, slot):
        side = slot ^ half
        return jnp.where(turn, ((p + 1 + 2 * half) & 3) * 2 + side, p + 4 * side)

    for step in range(3):
        p = (mine + step + 1) & 3
        for slot in range(2):
            for local in range(2):
                read = lambda start: far_ref[p, slot, start : start + 8, :]
                prepare(read, step * 4 + slot * 2 + local, local, xr, vr, by_row, masks)
    for level in range(1, LAYERS):
        for block in range(12):
            deepen(block, vr, level, masks)
    for slot in range(2):
        l = row_at(mine, slot)
        for n in range(8):
            sums[n, pl.ds(l, 1), :] = own_ref[slot * 8 + n : slot * 8 + n + 1, :]
    copy.wait()

    def some_pairs(step, carry):
        p, slot = (mine + step // 2 + 1) & 3, step % 2
        l = row_at(p, slot)
        blocks = []
        for n in range(8):
            rb = step * 2 + info[p, slot, n, base].astype(jnp.int32)
            blocks.append((rb, n * 2 + info[p, slot, n, base + 64].astype(jnp.int32)))
        for n, total in enumerate(pair_sums(blocks, xr, xc, vr, vc, masks)):
            sums[n, pl.ds(l, 1), :] = total
        return carry

    lax.fori_loop(0, 6, some_pairs, 0)

    tiles = []
    rows = jnp.zeros((8, 128), jnp.float32)
    for n in range(8):
        t = sums[n]
        for shift in (1, 2, 4, 8, 16):
            t = t + pltpu.roll(t, 128 - shift, 1)
        t = t * TILE_SCALE + SIGMA_B
        rows = jnp.where(lane >> 2 == n, jnp.take_along_axis(t, (lane & 3) * 32, axis=1), rows)
        tiles.append(jnp.take_along_axis(t, (lane & 1) * 64 + (lane & 2) * 16, axis=1))
    for n in range(8):
        tiles_out[n] = jnp.where(lane < 32, rows, tiles[n])


def order_kernel(tiles_ref, out_ref):
    high = lax.axis_index("wide") // 8
    for a in range(8):
        out_ref[a * 8 : a * 8 + 8, :] = tiles_ref[worker_narrow(a, high)]


def place_kernel(cols_ref, rows_ref, rows_out, cols_out, square):
    near = lax.axis_index("narrow")
    square[0:64, :] = cols_ref[...]
    square[64:72, :] = rows_ref[pl.ds(pl.multiple_of(near * 8, 8), 8), :]
    square[72:128, :] = jnp.zeros((56, 128), jnp.float32)
    turned = square[...].T
    cols_out[...] = turned[32:36, :64]
    lane = lane_iota()
    upper = jnp.where(sub_iota() >= 4, 1, 0)
    rows = jnp.zeros((8, 128), jnp.float32)
    for g in range(4):
        part = jnp.take_along_axis(turned[8 * g : 8 * g + 8, :], 64 + (lane & 7), axis=1)
        rows = jnp.where((lane >> 3) == 2 * g + upper, part, rows)
    rows_out[...] = (rows + pltpu.roll(rows, 4, 0))[:4, :64]


def f32(*shape):
    return jax.ShapeDtypeStruct(shape, jnp.float32)


def whole(count):
    return [pl.BlockSpec(memory_space=pltpu.VMEM)] * count


def params():
    return pltpu.CompilerParams(vmem_limit_bytes=32 * 1024 * 1024)


def call(kernel, outs, *args, scratch=()):
    return pl.pallas_call(
        kernel,
        out_shape=outs,
        in_specs=whole(len(args)),
        out_specs=tuple(whole(len(outs))) if isinstance(outs, tuple) else whole(1)[0],
        scratch_shapes=scratch,
        compiler_params=params(),
    )(*args)


def exchange(x, axis, groups=None):
    return lax.all_to_all(x, axis, split_axis=0, concat_axis=0, tiled=True, axis_index_groups=groups)


def shards(images, block_slot, pairs):
    vmem = lambda *shape: pltpu.VMEM(shape, jnp.float32)
    packed = call(
        pack_kernel,
        f32(8, ROWS, 128),
        images.transpose(1, 0, 2),
        block_slot.reshape(8, 128),
        pairs[0].T,
        scratch=[vmem(4 * CH, 8, 128), pltpu.VMEM((8, 128), jnp.int32)],
    )
    near = exchange(packed, "narrow")
    relayed = call(relay_kernel, f32(ROWS, 128), packed, near)
    first = lax.ppermute(relayed, BOTH, row_routes(0))
    second = lax.ppermute(relayed, BOTH, row_routes(1))
    xc, vc = call(col_kernel, (f32(16, 4 * CH, 8, 128), f32(16, 4 * LAYERS, 8, 128)), near)
    spread = call(spread_kernel, f32(4, 2, ROWS, 128), first, second)
    far = exchange(spread, "wide", low_groups())
    own = call(
        own_kernel,
        f32(16, 128),
        first,
        second,
        xc,
        vc,
        scratch=[
            vmem(4, 4 * CH, 8, 128),
            vmem(4, 4 * LAYERS, 8, 128),
            pltpu.SMEM((2, 8, 128), jnp.float32),
            pltpu.SemaphoreType.DMA((2,)),
        ],
    )
    tiles = call(
        tile_kernel,
        f32(8, 8, 128),
        far,
        own,
        xc,
        vc,
        scratch=[
            vmem(12, 4 * CH, 8, 128),
            vmem(12, 4 * LAYERS, 8, 128),
            vmem(8, 8, 128),
            pltpu.SMEM((4, 2, 8, 128), jnp.float32),
            pltpu.SemaphoreType.DMA,
        ],
    )
    ordered = call(order_kernel, f32(64, 128), exchange(tiles, "narrow"))
    rows, cols = call(
        place_kernel, (f32(4, 64), f32(4, 64)), ordered, exchange(ordered, "wide"), scratch=[vmem(128, 128)]
    )
    return rows.T[None], cols.T[None]


def solution(mesh):
    spec = P(BOTH, None, None)
    return jax.shard_map(
        shards, mesh=mesh, in_specs=(spec, P(), spec), out_specs=(spec, spec), check_vma=False
    )
```

time: 116 us -> 98.6 us (0.85)
  the two profiles are of different devices: /device:TPU:5 before, /device:TPU:1 now
where the time goes in v2:
time: 98.6 us; the launch traced here: 98.1 us
  blocking collectives  51 us (52%)
  starting transfers between devices  20.2 us (20%)
  waiting for transfers between devices  12.6 us (13%)
  Pallas kernels  12.2 us (12%)
  local copies, waits for them, and re-layouts  1.48 us (2%)
    all_to_all x3, blocking collectives, exchange(): lax.all_to_all(x, axis, split_axis=0, concat_axis=0, tiled=True, axis_ind...  51 us
    pallas_call x8, Pallas kernels, call(): pl.pallas_call(kernel, out_shape=outs, in_specs=whole(len(args)), out_spe...  12.2 us
    ppermute x1, starting transfers between devices, shards(): first = lax.ppermute(relayed, BOTH, row_routes(0))  11.4 us
    ppermute x1, waiting for transfers between devices, shards(): second = lax.ppermute(relayed, BOTH, row_routes(1))  8.56 us
    ppermute x1, starting transfers between devices, shards(): second = lax.ppermute(relayed, BOTH, row_routes(1))  5.29 us
    all_to_all x1, waiting for transfers between devices, exchange(): lax.all_to_all(x, axis, split_axis=0, concat_axis=0, tiled=True, axis_ind...  4.03 us
    all_to_all x1, starting transfers between devices, exchange(): lax.all_to_all(x, axis, split_axis=0, concat_axis=0, tiled=True, axis_ind...  3.46 us
  transfers between devices with their start and end apart: 3, of which 2 were waited for; matrix products, arithmetic and copies ran while one was open for 0% of the time, Pallas kernels for 4%

profile of v2, /device:TPU:1, one launch (start us, length us, event | category | flops | bytes accessed | tf_op | source)
XLA Modules:
  0.0 98.1 jit_solution(16432597704476192602)
XLA Ops:
  0.6 0.0 copy-start.1
  0.6 0.0 copy-start.2
  0.6 0.7 copy-done.1
  1.3 0.0 copy-done.2
  1.3 0.0 copy-start
  1.3 0.8 copy-done
  2.1 0.2 shard_map.50.own_ref
  2.3 17.7 %all_to_all.26.near_ref = f32[8,104,128]{2,1,0:T(8,128)S(1)} all-to-all(f32[8,104,128]{2,1,0:T(8,128)S(1)} %shard_map.50.own_ref), channel_id=1, replica_groups=mesh['wide'=64,'narrow'=8] {'narrow'}, dimensions={0} | all-to-all | bytes 851968 | tf_op jit(solution)/shard_map/all_to_all | solution.py:338
  20.0 11.4 %collective-permute-start = (f32[104,128]{1,0:T(8,128)S(1)}, f32[104,128]{1,0:T(8,128)S(1)}, u32[]{:S(2)}, u32[]{:S(2)}) collective-permute-start(f32[104,128]{1,0:T(8,128)S(1)} %shard_map.51), channel_id=1, source_target_pairs={{0,4},{1,92},{2,128},{3,216},{4,260},{5,348},{6,384},{7,472},{8,12... | collective-permute-start | bytes 159752 | tf_op jit(solution)/shard_map/ppermute | solution.py:353
  31.4 5.3 %collective-permute-start.1 = (f32[104,128]{1,0:T(8,128)S(1)}, f32[104,128]{1,0:T(8,128)S(1)}, u32[]{:S(2)}, u32[]{:S(2)}) collective-permute-start(f32[104,128]{1,0:T(8,128)S(1)} %shard_map.51), channel_id=1, source_target_pairs={{0,36},{1,108},{2,160},{3,232},{4,292},{5,364},{6,416},{7,488},{8,... | collective-permute-start | bytes 159752 | tf_op jit(solution)/shard_map/ppermute | solution.py:354
  36.7 0.0 collective-permute-done.first_ref
  36.7 8.6 %collective-permute-done.1.second_ref = f32[104,128]{1,0:T(8,128)S(1)} collective-permute-done((f32[104,128]{1,0:T(8,128)S(1)}, f32[104,128]{1,0:T(8,128)S(1)}, u32[]{:S(2)}, u32[]{:S(2)}) %collective-permute-start.1) | collective-permute-done | bytes 53280 | tf_op jit(solution)/shard_map/ppermute | solution.py:354
  45.2 0.8 shard_map.52
  46.0 3.5 %all-to-all-start.1 = ((f32[4,2,104,128]{3,2,1,0:T(8,128)}), f32[4,2,104,128]{3,2,1,0:T(8,128)S(1)}, u32[]{:S(2)}, u32[]{:S(2)}) async-start(f32[4,2,104,128]{3,2,1,0:T(8,128)} %shard_map.52), calls=%async_computation.1 | async-start | bytes 851968 | tf_op jit(solution)/shard_map/all_to_all | solution.py:338
  49.5 1.7 %shard_map.53 = (f32[16,12,8,128]{3,2,1,0:T(8,128)S(1)}, f32[16,16,8,128]{3,2,1,0:T(8,128)S(1)}) custom-call(f32[8,104,128]{2,1,0:T(8,128)S(1)} %all_to_all.26.near_ref), custom_call_target="tpu_custom_call" | custom-call | tf_op jit(solution)/shard_map/pallas_call | solution.py:327
  51.2 2.3 %shard_map.54.own_ref = f32[16,128]{1,0:T(8,128)S(1)} custom-call(f32[104,128]{1,0:T(8,128)S(1)} %collective-permute-done.first_ref, f32[104,128]{1,0:T(8,128)S(1)} %collective-permute-done.1.second_ref, f32[16,12,8,128]{3,2,1,0:T(8,128)S(1)} %get-tuple-element.6.xc, f32[16,16,8,128]{3,2,1,0:T(8,128)S(1)} %get-tuple-element.7.vc), custom_call_target="tpu_custom_call" | custom-call | tf_op jit(solution)/shard_map/pallas_call | solution.py:327
  53.5 4.0 %all-to-all-done.1.far_ref = f32[4,2,104,128]{3,2,1,0:T(8,128)S(1)} async-done(((f32[4,2,104,128]{3,2,1,0:T(8,128)}), f32[4,2,104,128]{3,2,1,0:T(8,128)S(1)}, u32[]{:S(2)}, u32[]{:S(2)}) %all-to-all-start.1) | async-done | bytes 426016 | tf_op jit(solution)/shard_map/all_to_all | solution.py:338
  57.5 6.5 %shard_map.55 = f32[8,8,128]{2,1,0:T(8,128)S(1)} custom-call(f32[4,2,104,128]{3,2,1,0:T(8,128)S(1)} %all-to-all-done.1.far_ref, f32[16,128]{1,0:T(8,128)S(1)} %shard_map.54.own_ref, f32[16,12,8,128]{3,2,1,0:T(8,128)S(1)} %get-tuple-element.6.xc, f32[16,16,8,128]{3,2,1,0:T(8,128)S(1)} %get-tuple-element.7.vc), custom_call_target="tpu_custom_call" | custom-call | tf_op jit(solution)/shard_map/pallas_call | solution.py:327
  64.1 12.7 %all_to_all.27.tiles_ref = f32[8,8,128]{2,1,0:T(8,128)S(1)} all-to-all(f32[8,8,128]{2,1,0:T(8,128)S(1)} %shard_map.55), channel_id=1, replica_groups=mesh['wide'=64,'narrow'=8] {'narrow'}, dimensions={0} | all-to-all | bytes 65536 | tf_op jit(solution)/shard_map/all_to_all | solution.py:338
  76.8 20.6 %all_to_all.28 = f32[64,1,128]{2,1,0:T(1,128)S(1)} all-to-all(f32[64,1,128]{2,1,0:T(1,128)S(1)} %bitcast.15), channel_id=1, replica_groups=mesh['wide'=64,'narrow'=8] {'wide'}, dimensions={0} | all-to-all | bytes 65536 | tf_op jit(solution)/shard_map/all_to_all | solution.py:338
  97.4 0.7 shard_map.57
  (2 shorter events, 0.0 us)
Async XLA Ops:
  0.6 0.7 copy-start.1
  0.6 0.7 copy-start.2
  1.3 0.8 copy-start
  20.0 16.7 %collective-permute-start = (f32[104,128]{1,0:T(8,128)S(1)}, f32[104,128]{1,0:T(8,128)S(1)}, u32[]{:S(2)}, u32[]{:S(2)}) collective-permute-start(f32[104,128]{1,0:T(8,128)S(1)} %shard_map.51), channel_id=1, source_target_pairs={{0,4},{1,92},{2,128},{3,216},{4,260},{5,348},{6,384},{7,472},{8,12... | collective-permute-start | bytes 159752 | tf_op jit(solution)/shard_map/ppermute | solution.py:353
  31.4 13.9 %collective-permute-start.1 = (f32[104,128]{1,0:T(8,128)S(1)}, f32[104,128]{1,0:T(8,128)S(1)}, u32[]{:S(2)}, u32[]{:S(2)}) collective-permute-start(f32[104,128]{1,0:T(8,128)S(1)} %shard_map.51), channel_id=1, source_target_pairs={{0,36},{1,108},{2,160},{3,232},{4,292},{5,364},{6,416},{7,488},{8,... | collective-permute-start | bytes 159752 | tf_op jit(solution)/shard_map/ppermute | solution.py:354
  46.0 11.5 %all-to-all-start.1 = ((f32[4,2,104,128]{3,2,1,0:T(8,128)}), f32[4,2,104,128]{3,2,1,0:T(8,128)S(1)}, u32[]{:S(2)}, u32[]{:S(2)}) async-start(f32[4,2,104,128]{3,2,1,0:T(8,128)} %shard_map.52), calls=%async_computation.1 | async-start | bytes 851968 | tf_op jit(solution)/shard_map/all_to_all | solution.py:338

commit v3 on v2

--- a/solution.py
+++ b/solution.py
@@ -57,6 +57,11 @@
         for l in range(8)
         for q in range(8)
     ]
+
+
+def home_groups():
+    order = [sorted(range(8), key=lambda a: worker_narrow(a, q)) for q in range(8)]
+    return [[flat(a, l, q) for a in order[q] for l in range(8)] for q in range(8)]
 
 
 def low_groups():
@@ -264,17 +269,18 @@
     copy.wait()
 
     def some_pairs(step, carry):
-        p, slot = (mine + step // 2 + 1) & 3, step % 2
-        l = row_at(p, slot)
-        blocks = []
-        for n in range(8):
-            rb = step * 2 + info[p, slot, n, base].astype(jnp.int32)
-            blocks.append((rb, n * 2 + info[p, slot, n, base + 64].astype(jnp.int32)))
-        for n, total in enumerate(pair_sums(blocks, xr, xc, vr, vc, masks)):
-            sums[n, pl.ds(l, 1), :] = total
+        p = (mine + step + 1) & 3
+        for slot in range(2):
+            l = row_at(p, slot)
+            blocks = []
+            for n in range(8):
+                rb = step * 4 + slot * 2 + info[p, slot, n, base].astype(jnp.int32)
+                blocks.append((rb, n * 2 + info[p, slot, n, base + 64].astype(jnp.int32)))
+            for n, total in enumerate(pair_sums(blocks, xr, xc, vr, vc, masks)):
+                sums[n, pl.ds(l, 1), :] = total
         return carry
 
-    lax.fori_loop(0, 6, some_pairs, 0)
+    lax.fori_loop(0, 3, some_pairs, 0)
 
     tiles = []
     rows = jnp.zeros((8, 128), jnp.float32)
@@ -289,16 +295,12 @@
         tiles_out[n] = jnp.where(lane < 32, rows, tiles[n])
 
 
-def order_kernel(tiles_ref, out_ref):
-    high = lax.axis_index("wide") // 8
+def place_kernel(tiles_ref, rows_ref, rows_out, cols_out, square):
+    high, near = lax.axis_index("wide") // 8, lax.axis_index("narrow")
     for a in range(8):
-        out_ref[a * 8 : a * 8 + 8, :] = tiles_ref[worker_narrow(a, high)]
-
-
-def place_kernel(cols_ref, rows_ref, rows_out, cols_out, square):
-    near = lax.axis_index("narrow")
-    square[0:64, :] = cols_ref[...]
-    square[64:72, :] = rows_ref[pl.ds(pl.multiple_of(near * 8, 8), 8), :]
+        square[a * 8 : a * 8 + 8, :] = tiles_ref[worker_narrow(a, high)]
+    start = pl.multiple_of(worker_narrow(near, near) * 8, 8)
+    square[64:72, :] = rows_ref[pl.ds(start, 8), :]
     square[72:128, :] = jnp.zeros((56, 128), jnp.float32)
     turned = square[...].T
     cols_out[...] = turned[32:36, :64]
@@ -384,10 +386,9 @@
             pltpu.SemaphoreType.DMA,
         ],
     )
-    ordered = call(order_kernel, f32(64, 128), exchange(tiles, "narrow"))
-    rows, cols = call(
-        place_kernel, (f32(4, 64), f32(4, 64)), ordered, exchange(ordered, "wide"), scratch=[vmem(128, 128)]
-    )
+    tiles = exchange(tiles, "narrow")
+    rows = exchange(tiles.reshape(64, 128), BOTH, home_groups())
+    rows, cols = call(place_kernel, (f32(4, 64), f32(4, 64)), tiles, rows, scratch=[vmem(128, 128)])
     return rows.T[None], cols.T[None]
 
 

time: 98.6 us -> 98.7 us (level)
    pallas_call x8 -> x7, Pallas kernels: 12.2 us -> 11.6 us  [call(): pl.pallas_call(kernel, out_shape=outs, in_specs=whole(len(args)), out_spe...]
where the time goes in v3:
time: 98.7 us; the launch traced here: 98 us
  blocking collectives  51.4 us (52%)
  starting transfers between devices  20.2 us (20%)
  waiting for transfers between devices  12.6 us (13%)
  Pallas kernels  11.6 us (12%)
  local copies, waits for them, and re-layouts  1.48 us (1%)
    all_to_all x3, blocking collectives, exchange(): lax.all_to_all(x, axis, split_axis=0, concat_axis=0, tiled=True, axis_ind...  51.4 us
    pallas_call x7, Pallas kernels, call(): pl.pallas_call(kernel, out_shape=outs, in_specs=whole(len(args)), out_spe...  11.6 us
    ppermute x1, starting transfers between devices, shards(): first = lax.ppermute(relayed, BOTH, row_routes(0))  11.4 us
    ppermute x1, waiting for transfers between devices, shards(): second = lax.ppermute(relayed, BOTH, row_routes(1))  8.56 us
    ppermute x1, starting transfers between devices, shards(): second = lax.ppermute(relayed, BOTH, row_routes(1))  5.29 us
    all_to_all x1, waiting for transfers between devices, exchange(): lax.all_to_all(x, axis, split_axis=0, concat_axis=0, tiled=True, axis_ind...  4.03 us
    all_to_all x1, starting transfers between devices, exchange(): lax.all_to_all(x, axis, split_axis=0, concat_axis=0, tiled=True, axis_ind...  3.46 us
  transfers between devices with their start and end apart: 3, of which 2 were waited for; matrix products, arithmetic and copies ran while one was open for 0% of the time, Pallas kernels for 4%

profile of v3, /device:TPU:1, one launch (start us, length us, event | category | flops | bytes accessed | tf_op | source)
XLA Modules:
  0.0 98.0 jit_solution(6914923415926119494)
XLA Ops:
  0.6 0.0 copy-start.1
  0.6 0.0 copy-start.2
  0.6 0.7 copy-done.1
  1.3 0.0 copy-done.2
  1.3 0.0 copy-start
  1.3 0.8 copy-done
  2.1 0.2 shard_map.50.own_ref
  2.3 17.7 %all_to_all.26.near_ref = f32[8,104,128]{2,1,0:T(8,128)S(1)} all-to-all(f32[8,104,128]{2,1,0:T(8,128)S(1)} %shard_map.50.own_ref), channel_id=1, replica_groups=mesh['wide'=64,'narrow'=8] {'narrow'}, dimensions={0} | all-to-all | bytes 851968 | tf_op jit(solution)/shard_map/all_to_all | solution.py:340
  20.0 11.4 %collective-permute-start = (f32[104,128]{1,0:T(8,128)S(1)}, f32[104,128]{1,0:T(8,128)S(1)}, u32[]{:S(2)}, u32[]{:S(2)}) collective-permute-start(f32[104,128]{1,0:T(8,128)S(1)} %shard_map.51), channel_id=1, source_target_pairs={{0,4},{1,92},{2,128},{3,216},{4,260},{5,348},{6,384},{7,472},{8,12... | collective-permute-start | bytes 159752 | tf_op jit(solution)/shard_map/ppermute | solution.py:355
  31.4 5.3 %collective-permute-start.1 = (f32[104,128]{1,0:T(8,128)S(1)}, f32[104,128]{1,0:T(8,128)S(1)}, u32[]{:S(2)}, u32[]{:S(2)}) collective-permute-start(f32[104,128]{1,0:T(8,128)S(1)} %shard_map.51), channel_id=1, source_target_pairs={{0,36},{1,108},{2,160},{3,232},{4,292},{5,364},{6,416},{7,488},{8,... | collective-permute-start | bytes 159752 | tf_op jit(solution)/shard_map/ppermute | solution.py:356
  36.7 0.0 collective-permute-done.first_ref
  36.7 8.6 %collective-permute-done.1.second_ref = f32[104,128]{1,0:T(8,128)S(1)} collective-permute-done((f32[104,128]{1,0:T(8,128)S(1)}, f32[104,128]{1,0:T(8,128)S(1)}, u32[]{:S(2)}, u32[]{:S(2)}) %collective-permute-start.1) | collective-permute-done | bytes 53280 | tf_op jit(solution)/shard_map/ppermute | solution.py:356
  45.2 0.8 shard_map.52
  46.0 3.5 %all-to-all-start.1 = ((f32[4,2,104,128]{3,2,1,0:T(8,128)}), f32[4,2,104,128]{3,2,1,0:T(8,128)S(1)}, u32[]{:S(2)}, u32[]{:S(2)}) async-start(f32[4,2,104,128]{3,2,1,0:T(8,128)} %shard_map.52), calls=%async_computation.1 | async-start | bytes 851968 | tf_op jit(solution)/shard_map/all_to_all | solution.py:340
  49.5 1.7 %shard_map.53 = (f32[16,12,8,128]{3,2,1,0:T(8,128)S(1)}, f32[16,16,8,128]{3,2,1,0:T(8,128)S(1)}) custom-call(f32[8,104,128]{2,1,0:T(8,128)S(1)} %all_to_all.26.near_ref), custom_call_target="tpu_custom_call" | custom-call | tf_op jit(solution)/shard_map/pallas_call | solution.py:329
  51.2 2.3 %shard_map.54.own_ref = f32[16,128]{1,0:T(8,128)S(1)} custom-call(f32[104,128]{1,0:T(8,128)S(1)} %collective-permute-done.first_ref, f32[104,128]{1,0:T(8,128)S(1)} %collective-permute-done.1.second_ref, f32[16,12,8,128]{3,2,1,0:T(8,128)S(1)} %get-tuple-element.6.xc, f32[16,16,8,128]{3,2,1,0:T(8,128)S(1)} %get-tuple-element.7.vc), custom_call_target="tpu_custom_call" | custom-call | tf_op jit(solution)/shard_map/pallas_call | solution.py:329
  53.5 4.0 %all-to-all-done.1.far_ref = f32[4,2,104,128]{3,2,1,0:T(8,128)S(1)} async-done(((f32[4,2,104,128]{3,2,1,0:T(8,128)}), f32[4,2,104,128]{3,2,1,0:T(8,128)S(1)}, u32[]{:S(2)}, u32[]{:S(2)}) %all-to-all-start.1) | async-done | bytes 426016 | tf_op jit(solution)/shard_map/all_to_all | solution.py:340
  57.5 5.9 %shard_map.55 = f32[8,8,128]{2,1,0:T(8,128)S(1)} custom-call(f32[4,2,104,128]{3,2,1,0:T(8,128)S(1)} %all-to-all-done.1.far_ref, f32[16,128]{1,0:T(8,128)S(1)} %shard_map.54.own_ref, f32[16,12,8,128]{3,2,1,0:T(8,128)S(1)} %get-tuple-element.6.xc, f32[16,16,8,128]{3,2,1,0:T(8,128)S(1)} %get-tuple-element.7.vc), custom_call_target="tpu_custom_call" | custom-call | tf_op jit(solution)/shard_map/pallas_call | solution.py:329
  63.5 12.7 %all_to_all.27.tiles_ref = f32[8,8,128]{2,1,0:T(8,128)S(1)} all-to-all(f32[8,8,128]{2,1,0:T(8,128)S(1)} %shard_map.55), channel_id=1, replica_groups=mesh['wide'=64,'narrow'=8] {'narrow'}, dimensions={0} | all-to-all | bytes 65536 | tf_op jit(solution)/shard_map/all_to_all | solution.py:340
  76.2 21.1 %all_to_all.28 = f32[64,1,128]{2,1,0:T(1,128)S(1)} all-to-all(f32[64,1,128]{2,1,0:T(1,128)S(1)} %bitcast.15), channel_id=1, replica_groups={{256,264,272,280,288,296,304,312,320,328,336,344,352,360,368,376,128,13..., dimensions={0} | all-to-all | bytes 65536 | tf_op jit(solution)/shard_map/all_to_all | solution.py:340
  97.3 0.7 shard_map.56
  (1 shorter events, 0.0 us)
Async XLA Ops:
  0.6 0.7 copy-start.1
  0.6 0.7 copy-start.2
  1.3 0.8 copy-start
  20.0 16.7 %collective-permute-start = (f32[104,128]{1,0:T(8,128)S(1)}, f32[104,128]{1,0:T(8,128)S(1)}, u32[]{:S(2)}, u32[]{:S(2)}) collective-permute-start(f32[104,128]{1,0:T(8,128)S(1)} %shard_map.51), channel_id=1, source_target_pairs={{0,4},{1,92},{2,128},{3,216},{4,260},{5,348},{6,384},{7,472},{8,12... | collective-permute-start | bytes 159752 | tf_op jit(solution)/shard_map/ppermute | solution.py:355
  31.4 13.9 %collective-permute-start.1 = (f32[104,128]{1,0:T(8,128)S(1)}, f32[104,128]{1,0:T(8,128)S(1)}, u32[]{:S(2)}, u32[]{:S(2)}) collective-permute-start(f32[104,128]{1,0:T(8,128)S(1)} %shard_map.51), channel_id=1, source_target_pairs={{0,36},{1,108},{2,160},{3,232},{4,292},{5,364},{6,416},{7,488},{8,... | collective-permute-start | bytes 159752 | tf_op jit(solution)/shard_map/ppermute | solution.py:356
  46.0 11.5 %all-to-all-start.1 = ((f32[4,2,104,128]{3,2,1,0:T(8,128)}), f32[4,2,104,128]{3,2,1,0:T(8,128)S(1)}, u32[]{:S(2)}, u32[]{:S(2)}) async-start(f32[4,2,104,128]{3,2,1,0:T(8,128)} %shard_map.52), calls=%async_computation.1 | async-start | bytes 851968 | tf_op jit(solution)/shard_map/all_to_all | solution.py:340
